TPU v7x, 32 devices: a whole 2x2x4 slice. The times are simulated.
32 devices in a mesh: groups: 2 (over x), patch: 16 (over z, y, core).
Axes of the slice: x: 2, y: 2, z: 4, core: 2. Of those that a mesh axis runs over, the one named last changes fastest.
Arguments:
- fine_latents: bfloat16 [20480, 512], P(('groups', 'patch')), parts along dimension 0, may hold values from -6 to 6
- coarse_latents: bfloat16 [5120, 512], P(('groups', 'patch')), parts along dimension 0, may hold values from -6 to 6
- up_weight: bfloat16 [512, 512], replicated, may hold values from -0.25 to 0.25
- down_weight: bfloat16 [512, 512], replicated, may hold values from -0.25 to 0.25
- fine_cotangent: bfloat16 [20480, 512], P(('groups', 'patch')), parts along dimension 0, may hold values from -6 to 6
- coarse_cotangent: bfloat16 [5120, 512], P(('groups', 'patch')), parts along dimension 0, may hold values from -6 to 6
- edge_fine: int32 [2, 24576], P(None, 'patch'), may hold values from 0 to 10239, as said below
- edge_coarse: int32 [2, 24576], P(None, 'patch'), may hold values from 0 to 2559, as said below
- block_counts: int32 [2, 384], P(None, 'patch'), may hold values from 16 to 64, as said below
Outputs:
- fine_grad: bfloat16 [20480, 512], P(('groups', 'patch')), parts along dimension 0
- coarse_grad: float32 [5120, 512], P(('groups', 'patch')), parts along dimension 0
- up_weight_grad: float32 [1024, 512], P(('groups', 'patch')), parts along dimension 0
- down_weight_grad: float32 [1024, 512], P(('groups', 'patch')), parts along dimension 0
There are 2 independent parts, one for each index of `groups`. A program takes and returns all parts, laid end to end along the dimension named above; an argument that names none is the same for every part. Nothing has to cross between parts.
Inputs may be any that keep to these rules, and one draw needn't show every extreme that they name: Edge row r, in either direction, belongs to patch r // 1536, and its fine node is one of that patch's nodes (edge_fine // 640 equals the patch). Within one patch's 1536 rows of a direction, the first 1024 rows name coarse nodes of the same patch (edge_coarse // 160), the next 256 rows those of the patch one lower, the last 256 rows those of the patch one higher, cyclically. `block_counts`: each patch has a full block in each direction.
All inputs are finite; a program needn't handle non-finite values.
Results may differ from a plain program's by a relative error of at most 0.01.
Values may be sent and summed in bfloat16 or wider, within the bound.
A program may use at most 64 MiB of HBM per device.

v0:
```python
import math

import jax
import jax.numpy as jnp
from jax import lax
from jax.sharding import PartitionSpec as P

NB_OWN = 16
NB_SIDE = 4


def passed_along(value, axis, steps):
    count = lax.axis_size(axis)
    pairs = [(source, (source + steps) % count) for source in range(count)]
    return lax.ppermute(value, axis, pairs)


def with_halo(array, sides, width):
    for axis, dim in sides:
        peers, length = (lax.axis_size(axis), array.shape[dim])
        up = [(i, (i + 1) % peers) for i in range(peers)]
        down = [(j, i) for i, j in up]
        last = lax.slice_in_dim(array, length - width, length, axis=dim)
        leading = lax.slice_in_dim(array, 0, width, axis=dim)
        before = lax.ppermute(last, axis, up)
        after = lax.ppermute(leading, axis, down)
        array = jnp.concatenate([before, array, after], axis=dim)
    return array


def silu_slope(values):
    sigm = jax.nn.sigmoid(values)
    return sigm * (1.0 + values * (1.0 - sigm))


def one_hot_rows(index, count):
    return (index[:, None] == jnp.arange(count, dtype=jnp.int32)[None, :]).astype(jnp.bfloat16)


def pick_rows(table, index):
    selector = one_hot_rows(index, table.shape[0])
    return jnp.dot(selector, table, preferred_element_type=jnp.float32).astype(table.dtype)


def add_rows(values, index, count):
    selector = one_hot_rows(index, count)
    upper = values.astype(jnp.bfloat16)
    lower = (values - upper.astype(jnp.float32)).astype(jnp.bfloat16)
    dims = (((0,), (0,)), ((), ()))
    total = lax.dot_general(selector, upper, dims, preferred_element_type=jnp.float32)
    return total + lax.dot_general(selector, lower, dims, preferred_element_type=jnp.float32)


def node_reply(table, step_by):
    return passed_along(table, "patch", step_by)


def edge_backward(gathered, weight, incoming):
    pre_act = jnp.dot(gathered, weight, preferred_element_type=jnp.float32)
    delta_b = (incoming * silu_slope(pre_act)).astype(jnp.bfloat16)
    weight_term = lax.dot_general(
        gathered, delta_b, (((0,), (0,)), ((), ())), preferred_element_type=jnp.float32
    )
    back_terms = lax.dot_general(
        delta_b, weight, (((1,), (1,)), ((), ())), preferred_element_type=jnp.float32
    )
    return (weight_term, back_terms)


def on_device(
    fine_latents,
    coarse_latents,
    up_weight,
    down_weight,
    fine_cotangent,
    coarse_cotangent,
    edge_fine,
    edge_coarse,
    block_counts,
):
    fine_count = fine_latents.shape[0]
    coarse_count = coarse_latents.shape[0]
    edge_count = edge_fine.shape[1]
    block_len = edge_count // block_counts.shape[1]
    patch_count = lax.axis_size("patch")
    my_index = lax.axis_index("patch")
    own_rows = NB_OWN * block_len
    side_rows = NB_SIDE * block_len
    positions = jnp.arange(edge_count, dtype=jnp.int32)
    count_rows = jnp.repeat(block_counts, block_len, axis=1)
    row_mask = ((positions % block_len)[None, :] < count_rows).astype(jnp.float32)
    fine_local = edge_fine - my_index * fine_count
    coarse_local = edge_coarse % coarse_count
    grad_scale = 1.0 / math.sqrt(patch_count * edge_count)
    region_base = jnp.where(
        positions < own_rows,
        coarse_count,
        jnp.where(positions < own_rows + side_rows, 0, 2 * coarse_count),
    )
    coarse_ext = with_halo(coarse_latents, (("patch", 0),), coarse_count)
    down_rows = pick_rows(coarse_ext, coarse_local[1] + region_base)
    down_in = pick_rows(fine_cotangent, fine_local[1]).astype(jnp.float32) * row_mask[1][:, None]
    down_term, down_back = edge_backward(down_rows, down_weight, down_in)
    node_acc = add_rows(down_back, coarse_local[1] + region_base, 3 * coarse_count)
    from_upper = node_reply(node_acc[:coarse_count], -1)
    from_lower = node_reply(node_acc[2 * coarse_count :], 1)
    coarse_sum = node_acc[coarse_count : 2 * coarse_count] + from_upper + from_lower
    coarse_grad = coarse_cotangent.astype(jnp.float32) + coarse_sum
    down_weight_grad = (
        lax.psum_scatter(down_term, "patch", scatter_dimension=0, tiled=True) * grad_scale
    )
    coarse_grad_b = coarse_grad.astype(jnp.bfloat16)
    grad_ext = with_halo(coarse_grad_b, (("patch", 0),), coarse_count)
    up_reads = pick_rows(grad_ext, coarse_local[0] + region_base)
    up_in = up_reads.astype(jnp.float32) * row_mask[0][:, None]
    up_rows = pick_rows(fine_latents, fine_local[0])
    up_term, up_back = edge_backward(up_rows, up_weight, up_in)
    fine_sum = add_rows(up_back, fine_local[0], fine_count)
    fine_grad = (fine_cotangent.astype(jnp.float32) + fine_sum).astype(jnp.bfloat16)
    up_weight_grad = (
        lax.psum_scatter(up_term, "patch", scatter_dimension=0, tiled=True) * grad_scale
    )
    return (fine_grad, coarse_grad, up_weight_grad, down_weight_grad)


def solution(mesh):
    return jax.shard_map(
        on_device,
        mesh=mesh,
        in_specs=(
            P(("groups", "patch"), None),
            P(("groups", "patch"), None),
            P(),
            P(),
            P(("groups", "patch"), None),
            P(("groups", "patch"), None),
            P(None, "patch"),
            P(None, "patch"),
            P(None, "patch"),
        ),
        out_specs=(
            P(("groups", "patch"), None),
            P(("groups", "patch"), None),
            P(("groups", "patch"), None),
            P(("groups", "patch"), None),
        ),
        check_vma=False,
    )
```

profile of v0, /device:TPU:0, one launch (start us, length us, event | category | flops | bytes accessed | tf_op | source)
XLA Modules:
  0.0 153.5 jit_solution(773849448216241676)
XLA Ops:
  7.2 0.5 collective-permute-start
  7.7 5.1 %collective-permute-start.1 = (bf16[160,512]{1,0:T(8,128)(2,1)}, bf16[160,512]{1,0:T(8,128)(2,1)S(1)}, u32[]{:S(2)}, u32[]{:S(2)}) collective-permute-start(bf16[160,512]{1,0:T(8,128)(2,1)} %param.10), channel_id=1, source_target_pairs={{1,0},{2,1},{3,2},{4,3},{5,4},{6,5},{7,6},{8,7},{9,8},{10,9},{11,1... | collective-permute-start | bytes 491528 | tf_op jit(solution)/shard_map/ppermute | solution.py:26
  12.8 0.7 broadcast_subtract_fusion
  13.5 0.7 and_select_fusion
  14.3 0.8 broadcast_in_dim.28
  15.2 2.6 %fusion.11 = bf16[1536,512]{1,0:T(8,128)(2,1)} fusion(bf16[640,512]{1,0:T(8,128)(2,1)S(1)} %copy-done, s32[1536]{0:T(1024)S(1)} %get-tuple-element.7), kind=kOutput, calls=%fused_computation.19 | convolution fusion | flops 1008402432 | bytes 2234368 | tf_op jit(solution)/shard_map/dot_general | solution.py:42
  17.9 1.0 fusion.9
  18.9 1.0 fusion.50
  19.9 0.1 copy-done.6
  20.0 2.8 %multiply_convert_fusion.1 = bf16[1536,512]{1,0:T(8,128)(2,1)S(1)} fusion(f32[1536,512]{1,0:T(8,128)S(1)} %fusion.50, bf16[640,512]{1,0:T(8,128)(2,1)S(1)} %copy-done.6, s32[1536]{0:T(1024)S(1)} %get-tuple-element.6, f32[1536]{0:T(1024)S(1)} %get-tuple-element.4), kind=kOutput, calls=%fused_computation.9 | convolution fusion | flops 1017053184 | bytes 5386240 | tf_op jit(solution)/shard_map/dot_general | solution.py:42
  22.8 2.0 %fusion.55 = f32[512,512]{1,0:T(8,128)} fusion(bf16[1536,512]{1,0:T(8,128)(2,1)S(1)} %fusion.9, bf16[1536,512]{1,0:T(8,128)(2,1)S(1)} %multiply_convert_fusion.1), kind=kOutput, calls=%fused_computation.79 | convolution fusion | flops 805306368 | bytes 4194304 | tf_op jit(solution)/shard_map/dot_general | solution.py:61
  24.8 2.7 %fusion.51 = f32[1536,512]{1,0:T(8,128)} fusion(bf16[1536,512]{1,0:T(8,128)(2,1)S(1)} %multiply_convert_fusion.1, bf16[512,512]{1,0:T(8,128)(2,1)S(1)} %copy-done.3), kind=kOutput, calls=%fused_computation.75 | convolution fusion | flops 805306368 | bytes 5242880 | tf_op jit(solution)/shard_map/dot_general | solution.py:64
  27.6 4.4 %fusion.4 = f32[480,512]{1,0:T(8,128)S(1)} fusion(f32[1536,512]{1,0:T(8,128)} %fusion.51, s32[1536]{0:T(1024)S(1)} %fusion.42), kind=kOutput, calls=%fused_computation.11 | convolution fusion | flops 758857728 | bytes 4134912 | tf_op jit(solution)/shard_map/dot_general | solution.py:51
  32.0 1.4 fusion.23
  33.4 2.6 %collective-permute-start.2 = (f32[160,512]{1,0:T(8,128)S(1)}, f32[160,512]{1,0:T(8,128)S(1)}, u32[]{:S(2)}, u32[]{:S(2)}) collective-permute-start(f32[160,512]{1,0:T(8,128)S(1)} %get-tuple-element.12), channel_id=1, source_target_pairs={{0,15},{1,0},{2,1},{3,2},{4,3},{5,4},{6,5},{7,6},{8,7},{9,8},{10,9... | collective-permute-start | bytes 983048 | tf_op jit(solution)/shard_map/ppermute | solution.py:15
  36.1 1.0 fusion.52
  37.0 3.6 %collective-permute-done.2 = f32[160,512]{1,0:T(8,128)S(1)} collective-permute-done((f32[160,512]{1,0:T(8,128)S(1)}, f32[160,512]{1,0:T(8,128)S(1)}, u32[]{:S(2)}, u32[]{:S(2)}) %collective-permute-start.2) | collective-permute-done | bytes 327712 | tf_op jit(solution)/shard_map/ppermute | solution.py:15
  40.6 4.6 %collective-permute-done.3 = f32[160,512]{1,0:T(8,128)S(1)} collective-permute-done((f32[160,512]{1,0:T(8,128)S(1)}, f32[160,512]{1,0:T(8,128)S(1)}, u32[]{:S(2)}, u32[]{:S(2)}) %collective-permute-start.3) | collective-permute-done | bytes 327712 | tf_op jit(solution)/shard_map/ppermute | solution.py:15
  45.2 0.8 fusion.47
  46.1 0.1 collective-permute-start.5
  46.2 0.4 collective-permute-start.4
  46.6 2.4 %collective-permute-done.5 = bf16[160,512]{1,0:T(8,128)(2,1)S(1)} collective-permute-done((bf16[160,512]{1,0:T(8,128)(2,1)S(1)}, bf16[160,512]{1,0:T(8,128)(2,1)S(1)}, u32[]{:S(2)}, u32[]{:S(2)}) %collective-permute-start.5) | collective-permute-done | bytes 163872 | tf_op jit(solution)/shard_map/ppermute | solution.py:26
  49.0 4.6 %collective-permute-done.4 = bf16[160,512]{1,0:T(8,128)(2,1)S(1)} collective-permute-done((bf16[160,512]{1,0:T(8,128)(2,1)S(1)}, bf16[160,512]{1,0:T(8,128)(2,1)S(1)}, u32[]{:S(2)}, u32[]{:S(2)}) %collective-permute-start.4) | collective-permute-done | bytes 163872 | tf_op jit(solution)/shard_map/ppermute | solution.py:25
  53.6 2.3 %multiply_convert_fusion = bf16[1536,512]{1,0:T(8,128)(2,1)S(1)} fusion(f32[1536,512]{1,0:T(8,128)S(1)} %fusion.52, f32[1536]{0:T(1024)S(1)} %get-tuple-element.5, s32[1536]{0:T(1024)S(1)} %fusion.43, bf16[160,512]{1,0:T(8,128)(2,1)S(1)} %collective-permute-done.5, bf16[160,512]{1,0:T(8,128)(2,1)S(1)} %get-tuple-element.10, ...), kind=kOutput, calls=%fused_computation.7 | convolution fusion | flops 766623744 | bytes 5222400 | tf_op jit(solution)/shard_map/dot_general | solution.py:42
  55.9 2.0 %fusion.54 = f32[512,512]{1,0:T(8,128)} fusion(bf16[1536,512]{1,0:T(8,128)(2,1)S(1)} %copy-done.1, bf16[1536,512]{1,0:T(8,128)(2,1)S(1)} %multiply_convert_fusion), kind=kOutput, calls=%fused_computation.78 | convolution fusion | flops 805306368 | bytes 4194304 | tf_op jit(solution)/shard_map/dot_general | solution.py:61
  57.9 1.0 fusion.53
  59.0 1.6 %fusion = f32[640,512]{1,0:T(8,128)S(1)} fusion(s32[1536]{0:T(1024)S(1)} %get-tuple-element.7, f32[1536,512]{1,0:T(8,128)S(1)} %fusion.53), kind=kOutput, calls=%fused_computation.2 | convolution fusion | flops 1010761728 | bytes 4462592 | tf_op jit(solution)/shard_map/dot_general | solution.py:51
  60.6 2.5 %fusion.22 = bf16[640,512]{1,0:T(8,128)(2,1)} fusion(f32[640,512]{1,0:T(8,128)S(1)} %fusion, s32[1536]{0:T(1024)S(1)} %get-tuple-element.7, bf16[640,512]{1,0:T(8,128)(2,1)S(1)} %copy-done.6, f32[1536,512]{1,0:T(8,128)S(1)} %fusion.53), kind=kOutput, calls=%fused_computation.30 | convolution fusion | flops 1009713152 | bytes 5773312 | tf_op jit(solution)/shard_map/dot_general | solution.py:50
  63.0 21.8 %reduce-scatter.5.cloned.1.call-done = f32[32,512]{1,0:T(8,128)} async-done(((f32[512,512]{1,0:T(8,128)}), f32[32,512]{1,0:T(8,128)}) %reduce-scatter.5.cloned.1.call-update) | async-done | bytes 65552 | tf_op jit(solution)/shard_map/reduce_scatter | solution.py:110
  84.8 1.5 broadcast_multiply_fusion
  86.3 59.0 %reduce-scatter.3.cloned.1.call-done = f32[32,512]{1,0:T(8,128)} async-done(((f32[512,512]{1,0:T(8,128)}), f32[32,512]{1,0:T(8,128)}) %reduce-scatter.3.cloned.1.call-update) | async-done | bytes 65552 | tf_op jit(solution)/shard_map/reduce_scatter | solution.py:121
  145.2 1.5 broadcast_multiply_fusion.1
  (31 shorter events, 0.4 us)
Async XLA Ops:
  7.2 8.0 %copy-start = (bf16[640,512]{1,0:T(8,128)(2,1)S(1)}, bf16[640,512]{1,0:T(8,128)(2,1)}, u32[]{:S(2)}) copy-start(bf16[640,512]{1,0:T(8,128)(2,1)} %param.9) | copy-start | bytes 1966084
  7.2 77.6 %reduce-scatter.5.cloned.1.call-start = ((), (), s32[]{:S(2)}) async-start(), calls=%async_computation.3 | async-start | bytes 1114112 | tf_op jit(solution)/shard_map/reduce_scatter | solution.py:110
  7.2 10.6 %collective-permute-start = (bf16[160,512]{1,0:T(8,128)(2,1)}, bf16[160,512]{1,0:T(8,128)(2,1)S(1)}, u32[]{:S(2)}, u32[]{:S(2)}) collective-permute-start(bf16[160,512]{1,0:T(8,128)(2,1)} %param.10), channel_id=1, source_target_pairs={{0,1},{1,2},{2,3},{3,4},{4,5},{5,6},{6,7},{7,8},{8,9},{9,10},{10,1... | collective-permute-start | bytes 491528 | tf_op jit(solution)/shard_map/ppermute | solution.py:25
  7.7 10.1 %collective-permute-start.1 = (bf16[160,512]{1,0:T(8,128)(2,1)}, bf16[160,512]{1,0:T(8,128)(2,1)S(1)}, u32[]{:S(2)}, u32[]{:S(2)}) collective-permute-start(bf16[160,512]{1,0:T(8,128)(2,1)} %param.10), channel_id=1, source_target_pairs={{1,0},{2,1},{3,2},{4,3},{5,4},{6,5},{7,6},{8,7},{9,8},{10,9},{11,1... | collective-permute-start | bytes 491528 | tf_op jit(solution)/shard_map/ppermute | solution.py:26
  15.2 2.7 %copy-start.7 = (bf16[160,512]{1,0:T(8,128)(2,1)S(1)}, bf16[160,512]{1,0:T(8,128)(2,1)}, u32[]{:S(2)}) copy-start(bf16[160,512]{1,0:T(8,128)(2,1)} %param.10) | copy-start | bytes 491524
  17.8 1.1 copy-start.3
  18.9 1.1 copy-start.6
  27.5 117.7 %reduce-scatter.3.cloned.1.call-start = ((), (), s32[]{:S(2)}) async-start(), calls=%async_computation.2 | async-start | bytes 1114112 | tf_op jit(solution)/shard_map/reduce_scatter | solution.py:121
  27.6 4.4 %copy-start.2 = (f32[1536,512]{1,0:T(8,128)S(1)}, f32[1536,512]{1,0:T(8,128)}, u32[]{:S(2)}) copy-start(f32[1536,512]{1,0:T(8,128)} %fusion.51) | copy-start | bytes 9437188
  31.9 4.1 %copy-start.1 = (bf16[1536,512]{1,0:T(8,128)(2,1)S(1)}, bf16[1536,512]{1,0:T(8,128)(2,1)}, u32[]{:S(2)}) copy-start(bf16[1536,512]{1,0:T(8,128)(2,1)} %fusion.11) | copy-start | bytes 4718596
  32.0 4.1 %copy-start.4 = (bf16[512,512]{1,0:T(8,128)(2,1)S(1)}, bf16[512,512]{1,0:T(8,128)(2,1)}, u32[]{:S(2)}) copy-start(bf16[512,512]{1,0:T(8,128)(2,1)} %param.11) | copy-start | bytes 1572868
  33.4 7.2 %collective-permute-start.2 = (f32[160,512]{1,0:T(8,128)S(1)}, f32[160,512]{1,0:T(8,128)S(1)}, u32[]{:S(2)}, u32[]{:S(2)}) collective-permute-start(f32[160,512]{1,0:T(8,128)S(1)} %get-tuple-element.12), channel_id=1, source_target_pairs={{0,15},{1,0},{2,1},{3,2},{4,3},{5,4},{6,5},{7,6},{8,7},{9,8},{10,9... | collective-permute-start | bytes 983048 | tf_op jit(solution)/shard_map/ppermute | solution.py:15
  36.0 9.2 %copy-start.5 = (bf16[160,512]{1,0:T(8,128)(2,1)S(1)}, bf16[160,512]{1,0:T(8,128)(2,1)}, u32[]{:S(2)}) copy-start(bf16[160,512]{1,0:T(8,128)(2,1)} %param.14) | copy-start | bytes 491524
  36.0 9.2 %collective-permute-start.3 = (f32[160,512]{1,0:T(8,128)S(1)}, f32[160,512]{1,0:T(8,128)S(1)}, u32[]{:S(2)}, u32[]{:S(2)}) collective-permute-start(f32[160,512]{1,0:T(8,128)S(1)} %get-tuple-element.13), channel_id=1, source_target_pairs={{0,1},{1,2},{2,3},{3,4},{4,5},{5,6},{6,7},{7,8},{8,9},{9,10},{10,1... | collective-permute-start | bytes 983048 | tf_op jit(solution)/shard_map/ppermute | solution.py:15
  46.1 2.9 %collective-permute-start.5 = (bf16[160,512]{1,0:T(8,128)(2,1)S(1)}, bf16[160,512]{1,0:T(8,128)(2,1)S(1)}, u32[]{:S(2)}, u32[]{:S(2)}) collective-permute-start(bf16[160,512]{1,0:T(8,128)(2,1)S(1)} %get-tuple-element.10), channel_id=1, source_target_pairs={{1,0},{2,1},{3,2},{4,3},{5,4},{6,5},{7,6},{8,7},{9,8},{10,9},{11,1... | collective-permute-start | bytes 491528 | tf_op jit(solution)/shard_map/ppermute | solution.py:26
  46.2 7.4 %collective-permute-start.4 = (bf16[160,512]{1,0:T(8,128)(2,1)S(1)}, bf16[160,512]{1,0:T(8,128)(2,1)S(1)}, u32[]{:S(2)}, u32[]{:S(2)}) collective-permute-start(bf16[160,512]{1,0:T(8,128)(2,1)S(1)} %get-tuple-element.10), channel_id=1, source_target_pairs={{0,1},{1,2},{2,3},{3,4},{4,5},{5,6},{6,7},{7,8},{8,9},{9,10},{10,1... | collective-permute-start | bytes 491528 | tf_op jit(solution)/shard_map/ppermute | solution.py:25
Sparse Core Ops, SparseCore 0:
  27.6 57.1 reduce-scatter.4
  88.8 56.3 reduce-scatter.2
where the time goes:
time: 154 us
  waiting for transfers between devices  96 us (62%)
  matrix products  28.1 us (18%)
  between operations  14.2 us (9%)
  starting transfers between devices  8.8 us (6%)
  other arithmetic  5.27 us (3%)
    reduce_scatter x1, waiting for transfers between devices, on_device(): lax.psum_scatter(up_term, 'patch', scatter_dimension=0, tiled=True)  59 us
    reduce_scatter x1, waiting for transfers between devices, on_device(): lax.psum_scatter(down_term, 'patch', scatter_dimension=0, tiled=True)  21.8 us
    dot_general x4, matrix products, pick_rows(): jnp.dot(selector, table, preferred_element_type=jnp.float32)  8.66 us
    ppermute x2, waiting for transfers between devices, passed_along(): return lax.ppermute(value, axis, pairs)  8.21 us
    dot_general x2, matrix products, add_rows(): lax.dot_general(selector, lower, dims, preferred_element_type=jnp.float32)  5.93 us
    ppermute x2, starting transfers between devices, with_halo(): after = lax.ppermute(leading, axis, down)  5.17 us
    ppermute x2, waiting for transfers between devices, with_halo(): before = lax.ppermute(last, axis, up)  4.61 us
    dot_general x2, matrix products, edge_backward(): lax.dot_general(gathered, delta_b, (((0,), (0,)), ((), ())), preferred_el...  4.01 us
  transfers between devices with their start and end apart: 8, of which 6 were waited for; matrix products, arithmetic and copies ran while one was open for 15% of the time, Pallas kernels for 0%

commit v1 on v0

v1 whole, which is shorter than its diff:
```python
import functools
import math

import jax
import jax.numpy as jnp
from jax import lax
from jax.experimental import pallas as pl
from jax.experimental.pallas import tpu as pltpu
from jax.sharding import PartitionSpec as P

NB_OWN = 16
NB_SIDE = 4
MESH = pl.DeviceIdType.MESH
F32 = jnp.float32
BF16 = jnp.bfloat16
NN = (((1,), (0,)), ((), ()))
NT = (((1,), (1,)), ((), ()))
TN = (((0,), (0,)), ((), ()))


def mm(a, b, dims):
    return lax.dot_general(a, b, dims, preferred_element_type=F32)


def silu_slope(values):
    sigm = 1.0 / (1.0 + jnp.exp(-values))
    return sigm * (1.0 + values * (1.0 - sigm))


def one_hot(index, count):
    rows = lax.broadcasted_iota(jnp.int32, (count, index.shape[1]), 0)
    return jnp.where(rows == index, 1.0, 0.0).astype(BF16)


def kernel(
    n,
    fine_ref,
    coarse_ref,
    up_w,
    down_w,
    fine_cot,
    coarse_cot,
    edge_fine,
    edge_coarse,
    counts,
    fine_out,
    coarse_out,
    up_out,
    down_out,
    u_send,
    u_recv,
    g_own,
    g_recv,
    slope_f,
    fine_t,
    adj_up,
    terms,
    half_recv,
    half_sum,
    peer_recv,
    halo_send_sem,
    halo_recv_sem,
    half_send_sem,
    half_recv_sem,
    peer_send_sem,
    peer_recv_sem,
):
    me = lax.axis_index("patch")
    lower, upper = lax.rem(me + n - 1, n), lax.rem(me + 1, n)
    chips = n // 2
    chip, core = me // 2, lax.rem(me, 2)
    partner = chip * 2 + (1 - core)
    fine_count, width = fine_ref.shape
    coarse_count = coarse_ref.shape[0]
    edge_count = edge_fine.shape[1]
    blocks = counts.shape[1]
    block_len = edge_count // blocks
    own_rows, side_rows = NB_OWN * block_len, NB_SIDE * block_len
    chunk = width // n
    scale = 1.0 / math.sqrt(n * edge_count)
    wire = terms.dtype

    def peer(k):
        return lax.rem(chip + k, chips) * 2 + core

    barrier = pltpu.get_barrier_semaphore()
    for device in [lower, upper] + [peer(k) for k in range(1, chips)]:
        pl.semaphore_signal(barrier, inc=1, device_id={"patch": device}, device_id_type=MESH)

    spread = lax.broadcasted_iota(jnp.int32, (blocks, edge_count), 1) // block_len
    spread = spread == lax.broadcasted_iota(jnp.int32, (blocks, edge_count), 0)
    spread = jnp.where(spread, 1.0, 0.0).astype(BF16)
    count_rows = mm(counts[...].astype(F32).astype(BF16), spread, NN)
    position = lax.broadcasted_iota(jnp.int32, (1, edge_count), 1) % block_len
    regions = (
        (0, own_rows, me),
        (own_rows, side_rows, lower),
        (own_rows + side_rows, side_rows, upper),
    )

    def selectors(direction, region):
        start, size, owner = region
        lanes = slice(start, start + size)
        valid = position[:, lanes] < count_rows[direction : direction + 1, lanes].astype(jnp.int32)
        coarse = edge_coarse[direction : direction + 1, lanes] - owner * coarse_count
        coarse = jnp.where(valid, coarse, -1)
        fine = edge_fine[direction : direction + 1, lanes] - me * fine_count
        return one_hot(coarse, coarse_count), one_hot(fine, fine_count)

    def gathered_sum(region):
        coarse_sel, fine_sel = selectors(1, region)
        adjacency = mm(coarse_sel, fine_sel, NT).astype(BF16)
        return mm(adjacency, fine_cot[...], NN)

    def remote(src, dst, send_sem, recv_sem, device):
        return pltpu.make_async_remote_copy(
            src_ref=src,
            dst_ref=dst,
            send_sem=send_sem,
            recv_sem=recv_sem,
            device_id={"patch": device},
            device_id_type=MESH,
        )

    u_copies = [
        remote(
            u_send.at[s], u_recv.at[s], halo_send_sem.at[s], halo_recv_sem.at[s], (lower, upper)[s]
        )
        for s in range(2)
    ]
    u_send[0] = gathered_sum(regions[1]).astype(BF16)
    pl.semaphore_wait(barrier, chips + 1)
    u_copies[0].start()
    u_send[1] = gathered_sum(regions[2]).astype(BF16)
    u_copies[1].start()

    u_sum = gathered_sum(regions[0])
    slope_c = silu_slope(mm(coarse_ref[...], down_w[...], NN))
    for i, region in enumerate(regions):
        coarse_sel, fine_sel = selectors(0, region)
        adj_up[i] = mm(fine_sel, coarse_sel, NT).astype(BF16)
    slope_f[...] = silu_slope(mm(fine_ref[...], up_w[...], NN))
    fine_t[...] = fine_ref[...].T

    for copy in u_copies:
        copy.wait()
    u_sum = u_sum + u_recv[0].astype(F32) + u_recv[1].astype(F32)
    delta_c = (slope_c * u_sum).astype(BF16)
    coarse_grad = coarse_cot[...].astype(F32) + mm(delta_c, down_w[...], NT)
    coarse_out[...] = coarse_grad
    g_own[...] = coarse_grad.astype(BF16)
    g_copies = [
        remote(
            g_own, g_recv.at[s], halo_send_sem.at[2 + s], halo_recv_sem.at[2 + s], (lower, upper)[s]
        )
        for s in range(2)
    ]
    for copy in g_copies:
        copy.start()

    def half_copy(which):
        return remote(
            terms.at[which, 1 - core],
            half_recv.at[which],
            half_send_sem.at[which],
            half_recv_sem.at[which],
            partner,
        )

    def put_term(which, term):
        term = term.reshape(chips, 2, chunk, width)
        for parity in range(2):
            terms[which, parity] = term[:, parity].astype(wire)
        half_copy(which).start()

    def peer_copy(which, k):
        return remote(
            half_sum.at[which, lax.rem(chip + k, chips)],
            peer_recv.at[which, k - 1],
            peer_send_sem.at[which, k - 1],
            peer_recv_sem.at[which, k - 1],
            peer(k),
        )

    def send_peers(which):
        half_copy(which).wait()
        total = terms[which, core].astype(F32) + half_recv[which].astype(F32)
        half_sum[which] = total.astype(wire)
        for k in range(1, chips):
            peer_copy(which, k).start()

    def finish(which, out_ref):
        total = half_sum[which, chip].astype(F32)
        for k in range(1, chips):
            peer_copy(which, k).wait()
            total = total + peer_recv[which, k - 1].astype(F32)
        out_ref[...] = total * scale

    put_term(0, mm(coarse_ref[...], delta_c, TN))
    v_sum = mm(adj_up[0], g_own[...], NN)
    for copy in g_copies:
        copy.wait()
    send_peers(0)
    v_sum = v_sum + mm(adj_up[1], g_recv[1], NN) + mm(adj_up[2], g_recv[0], NN)
    delta_f = (slope_f[...] * v_sum).astype(BF16)
    put_term(1, mm(fine_t[...], delta_f, NN))
    fine_sum = mm(delta_f, up_w[...], NT)
    fine_out[...] = (fine_cot[...].astype(F32) + fine_sum).astype(BF16)
    send_peers(1)
    finish(0, down_out)
    finish(1, up_out)


def on_device(
    fine_latents,
    coarse_latents,
    up_weight,
    down_weight,
    fine_cotangent,
    coarse_cotangent,
    edge_fine,
    edge_coarse,
    block_counts,
):
    n = lax.axis_size("patch")
    fine_count, width = fine_latents.shape
    coarse_count = coarse_latents.shape[0]
    chunk, chips = width // n, n // 2
    wire = BF16 if chunk % 16 == 0 else F32
    vmem = pl.BlockSpec(memory_space=pltpu.VMEM)
    dma = pltpu.SemaphoreType.DMA
    return pl.pallas_call(
        functools.partial(kernel, n),
        out_shape=(
            jax.ShapeDtypeStruct((fine_count, width), BF16),
            jax.ShapeDtypeStruct((coarse_count, width), F32),
            jax.ShapeDtypeStruct((chunk, width), F32),
            jax.ShapeDtypeStruct((chunk, width), F32),
        ),
        in_specs=[vmem] * 9,
        out_specs=[vmem] * 4,
        scratch_shapes=[
            pltpu.VMEM((2, coarse_count, width), BF16),
            pltpu.VMEM((2, coarse_count, width), BF16),
            pltpu.VMEM((coarse_count, width), BF16),
            pltpu.VMEM((2, coarse_count, width), BF16),
            pltpu.VMEM((fine_count, width), F32),
            pltpu.VMEM((width, fine_count), BF16),
            pltpu.VMEM((3, fine_count, coarse_count), BF16),
            pltpu.VMEM((2, 2, chips, chunk, width), wire),
            pltpu.VMEM((2, chips, chunk, width), wire),
            pltpu.VMEM((2, chips, chunk, width), wire),
            pltpu.VMEM((2, chips - 1, chunk, width), wire),
            dma((4,)),
            dma((4,)),
            dma((2,)),
            dma((2,)),
            dma((2, chips - 1)),
            dma((2, chips - 1)),
        ],
        compiler_params=pltpu.CompilerParams(
            collective_id=0, has_side_effects=True, vmem_limit_bytes=48 * 2**20
        ),
        cost_estimate=pl.CostEstimate(
            flops=4 * 10**9, bytes_accessed=4 * 10**6, transcendentals=4 * 10**5
        ),
    )(
        fine_latents,
        coarse_latents,
        up_weight,
        down_weight,
        fine_cotangent,
        coarse_cotangent,
        edge_fine,
        edge_coarse,
        block_counts,
    )


def solution(mesh):
    nodes = P(("groups", "patch"), None)
    edges = P(None, "patch")
    return jax.shard_map(
        on_device,
        mesh=mesh,
        in_specs=(nodes, nodes, P(), P(), nodes, nodes, edges, edges, edges),
        out_specs=(nodes, nodes, nodes, nodes),
        check_vma=False,
    )
```

time: 154 us -> 40.1 us (0.26)
  waiting for transfers between devices: 96 us -> 0 us
  matrix products: 28.1 us -> 0 us
  Pallas kernels: 0 us -> 28 us
  between operations: 14.2 us -> 0.66 us
  local copies, waits for them, and re-layouts: 1.12 us -> 11 us
  starting transfers between devices: 8.8 us -> 0 us
  other arithmetic: 5.27 us -> 0 us
    reduce_scatter x2 -> x0, waiting for transfers between devices: 80.7 us -> none  [the longest x1 59 us: on_device(): lax.psum_scatter(up_term, 'patch', scatter_dimension=0, tiled=True)]
    dot_general x14 -> x0, matrix products: 28.1 us -> none  [the longest x4 8.66 us: pick_rows(): jnp.dot(selector, table, preferred_element_type=jnp.float32)]
    pallas_call x0 -> x1, Pallas kernels: none -> 28 us  [on_device(): pl.pallas_call(functools.partial(kernel, n), out_shape=(jax.ShapeDtypeStr...]
    ppermute x6 -> x0, waiting for transfers between devices: 15.2 us -> none  [the longest x2 8.21 us: passed_along(): return lax.ppermute(value, axis, pairs)]
    unnamed x16 -> x22, local copies, waits for them, and re-layouts: 0.15 us -> 11 us
    ppermute x6 -> x0, starting transfers between devices: 8.72 us -> none  [the longest x2 5.17 us: with_halo(): after = lax.ppermute(leading, axis, down)]
    mul x2 -> x0, other arithmetic: 2.95 us -> none  [the longest x1 1.47 us: on_device(): lax.psum_scatter(down_term, 'patch', scatter_dimension=0, tiled=True)]
  transfers between devices with their start and end apart: 8 -> 0, of which waited for: 6 -> 0; matrix products, arithmetic and copies ran while one was open for 15% -> 0% of each run, Pallas kernels for 0% -> 0%
where the time goes in v1:
time: 40.1 us; the launch traced here: 39.6 us
  Pallas kernels  28 us (70%)
  local copies, waits for them, and re-layouts  11 us (27%)
  between operations  0.66 us (2%)
    pallas_call x1, Pallas kernels, on_device(): pl.pallas_call(functools.partial(kernel, n), out_shape=(jax.ShapeDtypeStr...  28 us
    unnamed x22, local copies, waits for them, and re-layouts  11 us

profile of v1, /device:TPU:0, one launch (start us, length us, event | category | flops | bytes accessed | tf_op | source)
XLA Modules:
  0.0 39.6 jit_solution(10983881047987389068)
XLA Ops:
  0.6 0.0 copy-start
  0.6 1.1 %copy-done = bf16[640,512]{1,0:T(8,128)(2,1)S(1)} copy-done((bf16[640,512]{1,0:T(8,128)(2,1)S(1)}, bf16[640,512]{1,0:T(8,128)(2,1)}, u32[]{:S(2)}) %copy-start) | copy-done | bytes 655384
  1.7 0.0 copy-start.1
  1.7 1.1 %copy-done.1 = bf16[640,512]{1,0:T(8,128)(2,1)S(1)} copy-done((bf16[640,512]{1,0:T(8,128)(2,1)S(1)}, bf16[640,512]{1,0:T(8,128)(2,1)}, u32[]{:S(2)}) %copy-start.1) | copy-done | bytes 655384
  2.8 0.0 copy-start.2
  2.8 1.0 %copy-done.2 = bf16[512,512]{1,0:T(8,128)(2,1)S(1)} copy-done((bf16[512,512]{1,0:T(8,128)(2,1)S(1)}, bf16[512,512]{1,0:T(8,128)(2,1)}, u32[]{:S(2)}) %copy-start.2) | copy-done | bytes 524312
  3.9 0.0 copy-start.3
  3.9 1.0 %copy-done.3 = bf16[512,512]{1,0:T(8,128)(2,1)S(1)} copy-done((bf16[512,512]{1,0:T(8,128)(2,1)S(1)}, bf16[512,512]{1,0:T(8,128)(2,1)}, u32[]{:S(2)}) %copy-start.3) | copy-done | bytes 524312
  4.9 0.0 copy-start.4
  4.9 0.9 %copy-done.4 = bf16[160,512]{1,0:T(8,128)(2,1)S(1)} copy-done((bf16[160,512]{1,0:T(8,128)(2,1)S(1)}, bf16[160,512]{1,0:T(8,128)(2,1)}, u32[]{:S(2)}) %copy-start.4) | copy-done | bytes 163864
  5.8 0.0 copy-start.5
  5.8 0.9 %copy-done.5 = bf16[160,512]{1,0:T(8,128)(2,1)S(1)} copy-done((bf16[160,512]{1,0:T(8,128)(2,1)S(1)}, bf16[160,512]{1,0:T(8,128)(2,1)}, u32[]{:S(2)}) %copy-start.5) | copy-done | bytes 163864
  6.7 0.0 copy-start.6
  6.7 0.7 %copy-done.6 = s32[2,1536]{1,0:T(2,128)S(1)} copy-done((s32[2,1536]{1,0:T(2,128)S(1)}, s32[2,1536]{1,0:T(2,128)}, u32[]{:S(2)}) %copy-start.6) | copy-done | bytes 12312
  7.4 0.0 copy-start.7
  7.4 0.7 %copy-done.7 = s32[2,1536]{1,0:T(2,128)S(1)} copy-done((s32[2,1536]{1,0:T(2,128)S(1)}, s32[2,1536]{1,0:T(2,128)}, u32[]{:S(2)}) %copy-start.7) | copy-done | bytes 12312
  8.1 0.0 copy-start.8
  8.1 0.7 %copy-done.8 = s32[2,24]{1,0:T(2,128)S(1)} copy-done((s32[2,24]{1,0:T(2,128)S(1)}, s32[2,24]{1,0:T(2,128)}, u32[]{:S(2)}) %copy-start.8) | copy-done | bytes 216
  8.8 28.0 %shard_map.120 = (bf16[640,512]{1,0:T(8,128)(2,1)S(1)}, f32[160,512]{1,0:T(8,128)S(1)}, f32[32,512]{1,0:T(8,128)S(1)}, f32[32,512]{1,0:T(8,128)S(1)}) custom-call(bf16[640,512]{1,0:T(8,128)(2,1)S(1)} %copy-done, bf16[160,512]{1,0:T(8,128)(2,1)S(1)} %copy-done.4, bf16[512,512]{1,0:T(8,128)(2,1)S(1)} %copy-done.2, bf16[512,512]{1,0:T(8,128)(2,1)S(1)} %copy-done.3, ...), custom_call_target="tpu_custom_call" | custom-call | flops 4000000000 | bytes 4000000 | tf_op jit(solution)/shard_map/pallas_call | solution.py:232
  36.8 0.8 %copy.17 = bf16[640,512]{1,0:T(8,128)(2,1)} copy(bf16[640,512]{1,0:T(8,128)(2,1)S(1)} %get-tuple-element.8) | data formatting | bytes 1310720
  37.6 0.7 %copy.18 = f32[160,512]{1,0:T(8,128)} copy(f32[160,512]{1,0:T(8,128)S(1)} %get-tuple-element.9) | data formatting | bytes 655360
  38.4 0.6 %copy.19 = f32[32,512]{1,0:T(8,128)} copy(f32[32,512]{1,0:T(8,128)S(1)} %get-tuple-element.10) | data formatting | bytes 131072
  39.0 0.6 %copy.20 = f32[32,512]{1,0:T(8,128)} copy(f32[32,512]{1,0:T(8,128)S(1)} %get-tuple-element.11) | data formatting | bytes 131072
Async XLA Ops:
  0.6 1.1 %copy-start = (bf16[640,512]{1,0:T(8,128)(2,1)S(1)}, bf16[640,512]{1,0:T(8,128)(2,1)}, u32[]{:S(2)}) copy-start(bf16[640,512]{1,0:T(8,128)(2,1)} %fine_ref.1) | copy-start | bytes 1966084
  1.7 1.1 %copy-start.1 = (bf16[640,512]{1,0:T(8,128)(2,1)S(1)}, bf16[640,512]{1,0:T(8,128)(2,1)}, u32[]{:S(2)}) copy-start(bf16[640,512]{1,0:T(8,128)(2,1)} %fine_cot.1) | copy-start | bytes 1966084
  2.8 1.0 %copy-start.2 = (bf16[512,512]{1,0:T(8,128)(2,1)S(1)}, bf16[512,512]{1,0:T(8,128)(2,1)}, u32[]{:S(2)}) copy-start(bf16[512,512]{1,0:T(8,128)(2,1)} %up_w.1) | copy-start | bytes 1572868
  3.9 1.0 %copy-start.3 = (bf16[512,512]{1,0:T(8,128)(2,1)S(1)}, bf16[512,512]{1,0:T(8,128)(2,1)}, u32[]{:S(2)}) copy-start(bf16[512,512]{1,0:T(8,128)(2,1)} %down_w.1) | copy-start | bytes 1572868
  4.9 0.9 %copy-start.4 = (bf16[160,512]{1,0:T(8,128)(2,1)S(1)}, bf16[160,512]{1,0:T(8,128)(2,1)}, u32[]{:S(2)}) copy-start(bf16[160,512]{1,0:T(8,128)(2,1)} %coarse_ref.1) | copy-start | bytes 491524
  5.8 0.9 %copy-start.5 = (bf16[160,512]{1,0:T(8,128)(2,1)S(1)}, bf16[160,512]{1,0:T(8,128)(2,1)}, u32[]{:S(2)}) copy-start(bf16[160,512]{1,0:T(8,128)(2,1)} %coarse_cot.1) | copy-start | bytes 491524
  6.7 0.7 %copy-start.6 = (s32[2,1536]{1,0:T(2,128)S(1)}, s32[2,1536]{1,0:T(2,128)}, u32[]{:S(2)}) copy-start(s32[2,1536]{1,0:T(2,128)} %edge_fine.1) | copy-start | bytes 36868
  7.4 0.7 %copy-start.7 = (s32[2,1536]{1,0:T(2,128)S(1)}, s32[2,1536]{1,0:T(2,128)}, u32[]{:S(2)}) copy-start(s32[2,1536]{1,0:T(2,128)} %edge_coarse.1) | copy-start | bytes 36868
  8.1 0.7 %copy-start.8 = (s32[2,24]{1,0:T(2,128)S(1)}, s32[2,24]{1,0:T(2,128)}, u32[]{:S(2)}) copy-start(s32[2,24]{1,0:T(2,128)} %counts.1) | copy-start | bytes 580

commit v2 on v1

--- a/solution.py
+++ b/solution.py
@@ -10,6 +10,7 @@
 
 NB_OWN = 16
 NB_SIDE = 4
+VMEM_LIMIT = 61 * 2**20
 MESH = pl.DeviceIdType.MESH
 F32 = jnp.float32
 BF16 = jnp.bfloat16
@@ -34,6 +35,19 @@
 
 def kernel(
     n,
+    fine_hbm,
+    coarse_hbm,
+    up_w_hbm,
+    down_w_hbm,
+    fine_cot_hbm,
+    coarse_cot_hbm,
+    edge_fine_hbm,
+    edge_coarse_hbm,
+    counts_hbm,
+    fine_hbm_out,
+    coarse_hbm_out,
+    up_hbm_out,
+    down_hbm_out,
     fine_ref,
     coarse_ref,
     up_w,
@@ -43,10 +57,12 @@
     edge_fine,
     edge_coarse,
     counts,
+    load_sem,
     fine_out,
     coarse_out,
     up_out,
     down_out,
+    store_sem,
     u_send,
     u_recv,
     g_own,
@@ -83,10 +99,41 @@
     def peer(k):
         return lax.rem(chip + k, chips) * 2 + core
 
+    loads = [
+        pltpu.make_async_copy(src, dst, load_sem.at[i])
+        for i, (src, dst) in enumerate(
+            (
+                (counts_hbm, counts),
+                (edge_coarse_hbm, edge_coarse),
+                (edge_fine_hbm, edge_fine),
+                (fine_cot_hbm, fine_cot),
+                (down_w_hbm, down_w),
+                (coarse_hbm, coarse_ref),
+                (coarse_cot_hbm, coarse_cot),
+                (fine_hbm, fine_ref),
+                (up_w_hbm, up_w),
+            )
+        )
+    ]
+    for copy in loads:
+        copy.start()
+    stores = [
+        pltpu.make_async_copy(src, dst, store_sem.at[i])
+        for i, (src, dst) in enumerate(
+            (
+                (fine_out, fine_hbm_out),
+                (coarse_out, coarse_hbm_out),
+                (up_out, up_hbm_out),
+                (down_out, down_hbm_out),
+            )
+        )
+    ]
     barrier = pltpu.get_barrier_semaphore()
     for device in [lower, upper] + [peer(k) for k in range(1, chips)]:
         pl.semaphore_signal(barrier, inc=1, device_id={"patch": device}, device_id_type=MESH)
 
+    for copy in loads[:3]:
+        copy.wait()
     spread = lax.broadcasted_iota(jnp.int32, (blocks, edge_count), 1) // block_len
     spread = spread == lax.broadcasted_iota(jnp.int32, (blocks, edge_count), 0)
     spread = jnp.where(spread, 1.0, 0.0).astype(BF16)
@@ -107,10 +154,9 @@
         fine = edge_fine[direction : direction + 1, lanes] - me * fine_count
         return one_hot(coarse, coarse_count), one_hot(fine, fine_count)
 
-    def gathered_sum(region):
+    def down_adjacency(region):
         coarse_sel, fine_sel = selectors(1, region)
-        adjacency = mm(coarse_sel, fine_sel, NT).astype(BF16)
-        return mm(adjacency, fine_cot[...], NN)
+        return mm(coarse_sel, fine_sel, NT).astype(BF16)
 
     def remote(src, dst, send_sem, recv_sem, device):
         return pltpu.make_async_remote_copy(
@@ -128,19 +174,20 @@
         )
         for s in range(2)
     ]
-    u_send[0] = gathered_sum(regions[1]).astype(BF16)
+    adj_lower, adj_upper = down_adjacency(regions[1]), down_adjacency(regions[2])
+    loads[3].wait()
+    u_send[0] = mm(adj_lower, fine_cot[...], NN).astype(BF16)
     pl.semaphore_wait(barrier, chips + 1)
     u_copies[0].start()
-    u_send[1] = gathered_sum(regions[2]).astype(BF16)
+    u_send[1] = mm(adj_upper, fine_cot[...], NN).astype(BF16)
     u_copies[1].start()
 
-    u_sum = gathered_sum(regions[0])
+    u_sum = mm(down_adjacency(regions[0]), fine_cot[...], NN)
+    for copy in loads[4:]:
+        copy.wait()
     slope_c = silu_slope(mm(coarse_ref[...], down_w[...], NN))
-    for i, region in enumerate(regions):
-        coarse_sel, fine_sel = selectors(0, region)
-        adj_up[i] = mm(fine_sel, coarse_sel, NT).astype(BF16)
+    fine_t[...] = fine_ref[...].T
     slope_f[...] = silu_slope(mm(fine_ref[...], up_w[...], NN))
-    fine_t[...] = fine_ref[...].T
 
     for copy in u_copies:
         copy.wait()
@@ -157,6 +204,7 @@
     ]
     for copy in g_copies:
         copy.start()
+    stores[1].start()
 
     def half_copy(which):
         return remote(
@@ -197,6 +245,9 @@
         out_ref[...] = total * scale
 
     put_term(0, mm(coarse_ref[...], delta_c, TN))
+    for i, region in enumerate(regions):
+        coarse_sel, fine_sel = selectors(0, region)
+        adj_up[i] = mm(fine_sel, coarse_sel, NT).astype(BF16)
     v_sum = mm(adj_up[0], g_own[...], NN)
     for copy in g_copies:
         copy.wait()
@@ -206,9 +257,26 @@
     put_term(1, mm(fine_t[...], delta_f, NN))
     fine_sum = mm(delta_f, up_w[...], NT)
     fine_out[...] = (fine_cot[...].astype(F32) + fine_sum).astype(BF16)
+    stores[0].start()
     send_peers(1)
     finish(0, down_out)
+    stores[3].start()
     finish(1, up_out)
+    stores[2].start()
+    for copy in stores:
+        copy.wait()
+
+
+def store_kernel(*refs):
+    count = len(refs) // 2
+    sems = refs[-1]
+    copies = [
+        pltpu.make_async_copy(refs[i], refs[count + i], sems.at[i]) for i in range(count)
+    ]
+    for copy in copies:
+        copy.start()
+    for copy in copies:
+        copy.wait()
 
 
 def on_device(
@@ -227,19 +295,37 @@
     coarse_count = coarse_latents.shape[0]
     chunk, chips = width // n, n // 2
     wire = BF16 if chunk % 16 == 0 else F32
-    vmem = pl.BlockSpec(memory_space=pltpu.VMEM)
+    hbm = pl.BlockSpec(memory_space=pltpu.HBM)
     dma = pltpu.SemaphoreType.DMA
-    return pl.pallas_call(
+    arguments = (
+        fine_latents,
+        coarse_latents,
+        up_weight,
+        down_weight,
+        fine_cotangent,
+        coarse_cotangent,
+        edge_fine,
+        edge_coarse,
+        block_counts,
+    )
+    out_shape = (
+        jax.ShapeDtypeStruct((fine_count, width), BF16),
+        jax.ShapeDtypeStruct((coarse_count, width), F32),
+        jax.ShapeDtypeStruct((chunk, width), F32),
+        jax.ShapeDtypeStruct((chunk, width), F32),
+    )
+    results = pl.pallas_call(
         functools.partial(kernel, n),
-        out_shape=(
-            jax.ShapeDtypeStruct((fine_count, width), BF16),
-            jax.ShapeDtypeStruct((coarse_count, width), F32),
-            jax.ShapeDtypeStruct((chunk, width), F32),
-            jax.ShapeDtypeStruct((chunk, width), F32),
-        ),
-        in_specs=[vmem] * 9,
-        out_specs=[vmem] * 4,
-        scratch_shapes=[
+        out_shape=out_shape,
+        in_specs=[hbm] * 9,
+        out_specs=[hbm] * 4,
+        scratch_shapes=[pltpu.VMEM(value.shape, value.dtype) for value in arguments]
+        + [
+            dma((9,)),
+        ]
+        + [pltpu.VMEM(value.shape, value.dtype) for value in out_shape]
+        + [
+            dma((4,)),
             pltpu.VMEM((2, coarse_count, width), BF16),
             pltpu.VMEM((2, coarse_count, width), BF16),
             pltpu.VMEM((coarse_count, width), BF16),
@@ -259,22 +345,20 @@
             dma((2, chips - 1)),
         ],
         compiler_params=pltpu.CompilerParams(
-            collective_id=0, has_side_effects=True, vmem_limit_bytes=48 * 2**20
+            collective_id=0, has_side_effects=True, vmem_limit_bytes=VMEM_LIMIT
         ),
         cost_estimate=pl.CostEstimate(
             flops=4 * 10**9, bytes_accessed=4 * 10**6, transcendentals=4 * 10**5
         ),
-    )(
-        fine_latents,
-        coarse_latents,
-        up_weight,
-        down_weight,
-        fine_cotangent,
-        coarse_cotangent,
-        edge_fine,
-        edge_coarse,
-        block_counts,
-    )
+    )(*arguments)
+    return pl.pallas_call(
+        store_kernel,
+        out_shape=out_shape,
+        in_specs=[hbm] * 4,
+        out_specs=[hbm] * 4,
+        scratch_shapes=[dma((4,))],
+        compiler_params=pltpu.CompilerParams(vmem_limit_bytes=VMEM_LIMIT),
+    )(*results)
 
 
 def solution(mesh):

time: 40.1 us -> 63.8 us (1.59)
  Pallas kernels: 28 us -> 63.1 us
  local copies, waits for them, and re-layouts: 11 us -> 0 us
    pallas_call x1 -> x2, Pallas kernels: 28 us -> 63.1 us  [the longest x1 34.9 us: on_device(): pl.pallas_call(store_kernel, out_shape=out_shape, in_specs=[hbm] * 4, out...]
    unnamed x22 -> x0, local copies, waits for them, and re-layouts: 11 us -> none
where the time goes in v2:
time: 63.8 us; the launch traced here: 63.7 us
  Pallas kernels  63.1 us (99%)
  between operations  0.64 us (1%)
    pallas_call x1, Pallas kernels, on_device(): pl.pallas_call(store_kernel, out_shape=out_shape, in_specs=[hbm] * 4, out...  34.9 us
    pallas_call x1, Pallas kernels, on_device(): pl.pallas_call(functools.partial(kernel, n), out_shape=out_shape, in_spec...  28.2 us

profile of v2, /device:TPU:0, one launch (start us, length us, event | category | flops | bytes accessed | tf_op | source)
XLA Modules:
  0.0 63.7 jit_solution(12714969259295158453)
XLA Ops:
  0.6 28.2 %shard_map.120 = (bf16[640,512]{1,0:T(8,128)(2,1)}, f32[160,512]{1,0:T(8,128)}, f32[32,512]{1,0:T(8,128)}, f32[32,512]{1,0:T(8,128)}) custom-call(bf16[640,512]{1,0:T(8,128)(2,1)} %fine_hbm.1, bf16[160,512]{1,0:T(8,128)(2,1)} %coarse_hbm.1, bf16[512,512]{1,0:T(8,128)(2,1)} %up_w_hbm.1, bf16[512,512]{1,0:T(8,128)(2,1)} %down_w_hbm.1, ...), custom_call_target="tpu_custom_call" | custom-call | flops 4000000000 | bytes 4000000 | tf_op jit(solution)/shard_map/pallas_call | solution.py:317
  28.8 34.9 %shard_map.121 = (bf16[640,512]{1,0:T(8,128)(2,1)}, f32[160,512]{1,0:T(8,128)}, f32[32,512]{1,0:T(8,128)}, f32[32,512]{1,0:T(8,128)}) custom-call(bf16[640,512]{1,0:T(8,128)(2,1)} %get-tuple-element.8.refs_0_, f32[160,512]{1,0:T(8,128)} %get-tuple-element.9.refs_1_, f32[32,512]{1,0:T(8,128)} %get-tuple-element.10.refs_2_, f32[32,512]{1,0:T(8,128)} %get-tuple-element.11.refs_3_), custom_call_target="tpu_custom_call" | custom-call | tf_op jit(solution)/shard_map/pallas_call | solution.py:354

commit v3 on v2

--- a/solution.py
+++ b/solution.py
@@ -268,14 +268,22 @@
 
 
 def store_kernel(*refs):
-    count = len(refs) // 2
-    sems = refs[-1]
-    copies = [
-        pltpu.make_async_copy(refs[i], refs[count + i], sems.at[i]) for i in range(count)
-    ]
-    for copy in copies:
+    sources, results, stages = refs[:4], refs[4:8], refs[8:12]
+    load_sem, save_sem = refs[12:]
+    loads = [
+        pltpu.make_async_copy(src, stage, load_sem.at[i])
+        for i, (src, stage) in enumerate(zip(sources, stages))
+    ]
+    saves = [
+        pltpu.make_async_copy(stage, dst, save_sem.at[i])
+        for i, (stage, dst) in enumerate(zip(stages, results))
+    ]
+    for copy in loads:
         copy.start()
-    for copy in copies:
+    for load, save in zip(loads[::-1], saves[::-1]):
+        load.wait()
+        save.start()
+    for copy in saves:
         copy.wait()
 
 
@@ -356,7 +364,8 @@
         out_shape=out_shape,
         in_specs=[hbm] * 4,
         out_specs=[hbm] * 4,
-        scratch_shapes=[dma((4,))],
+        scratch_shapes=[pltpu.VMEM(value.shape, value.dtype) for value in out_shape]
+        + [dma((4,)), dma((4,))],
         compiler_params=pltpu.CompilerParams(vmem_limit_bytes=VMEM_LIMIT),
     )(*results)
 

time: 63.8 us -> 31.2 us (0.49)
  Pallas kernels: 63.1 us -> 30.4 us
    pallas_call x1, Pallas kernels: 34.9 us -> 2.22 us  [on_device(): pl.pallas_call(store_kernel, out_shape=out_shape, in_specs=[hbm] * 4, out...]
where the time goes in v3:
time: 31.2 us; the launch traced here: 31 us
  Pallas kernels  30.4 us (97%)
  between operations  0.64 us (2%)
    pallas_call x1, Pallas kernels, on_device(): pl.pallas_call(functools.partial(kernel, n), out_shape=out_shape, in_spec...  28.2 us
    pallas_call x1, Pallas kernels, on_device(): pl.pallas_call(store_kernel, out_shape=out_shape, in_specs=[hbm] * 4, out...  2.22 us

profile of v3, /device:TPU:0, one launch (start us, length us, event | category | flops | bytes accessed | tf_op | source)
XLA Modules:
  0.0 31.0 jit_solution(1745936275207589850)
XLA Ops:
  0.6 28.2 %shard_map.120 = (bf16[640,512]{1,0:T(8,128)(2,1)}, f32[160,512]{1,0:T(8,128)}, f32[32,512]{1,0:T(8,128)}, f32[32,512]{1,0:T(8,128)}) custom-call(bf16[640,512]{1,0:T(8,128)(2,1)} %fine_hbm.1, bf16[160,512]{1,0:T(8,128)(2,1)} %coarse_hbm.1, bf16[512,512]{1,0:T(8,128)(2,1)} %up_w_hbm.1, bf16[512,512]{1,0:T(8,128)(2,1)} %down_w_hbm.1, ...), custom_call_target="tpu_custom_call" | custom-call | flops 4000000000 | bytes 4000000 | tf_op jit(solution)/shard_map/pallas_call | solution.py:325
  28.8 2.2 %shard_map.121 = (bf16[640,512]{1,0:T(8,128)(2,1)}, f32[160,512]{1,0:T(8,128)}, f32[32,512]{1,0:T(8,128)}, f32[32,512]{1,0:T(8,128)}) custom-call(bf16[640,512]{1,0:T(8,128)(2,1)} %get-tuple-element.8.refs_0_, f32[160,512]{1,0:T(8,128)} %get-tuple-element.9.refs_1_, f32[32,512]{1,0:T(8,128)} %get-tuple-element.10.refs_2_, f32[32,512]{1,0:T(8,128)} %get-tuple-element.11.refs_3_), custom_call_target="tpu_custom_call" | custom-call | tf_op jit(solution)/shard_map/pallas_call | solution.py:362
